TPU v7x, 512 devices: a whole 4x4x16 slice. The times are simulated.
512 devices in a mesh: grp: 4 (over y), dev: 128 (over z, x, core).
Axes of the slice: x: 4, y: 4, z: 16, core: 2. Of those that a mesh axis runs over, the one named last changes fastest.
Arguments:
- embeddings: bfloat16 [131072, 768], P(('grp', 'dev')), parts along dimension 0, may hold values from -80 to 80, as said below
- block_ids: int32 [131072], P(('grp', 'dev')), parts along dimension 0, may hold values from 0 to 127, as said below
Outputs:
- maxima: float32 [131072], P(('grp', 'dev')), parts along dimension 0
There are 4 independent parts, one for each index of `grp`. A program takes and returns all parts, laid end to end along the dimension named above; each array names one. Nothing has to cross between parts.
Inputs may be any that keep to these rules, and one draw needn't show every extreme that they name: `block_ids`: at most 4 rows of one device name one block; every block is named by at least one row of every device; in every draw one block is named by 4 rows of every device. `embeddings`: no row is zero.
All inputs are finite; a program needn't handle non-finite values.
Results may differ from a plain program's by a relative error of at most 0.00049.
Values may be sent and summed in bfloat16 or wider, within the bound.
No kernel may reach another device: no remote copies, remote signals or barrier semaphores. Data moves between devices by JAX's collectives and lax.ppermute only.
A program may use at most 64 MiB of HBM per device.

v0:
```python
import jax
import jax.numpy as jnp
from jax import lax
from jax.sharding import PartitionSpec as P


def from_partner(block, axis, distance):
    count = lax.axis_size(axis)
    route = []
    for low in range(count):
        high = low | 1 << distance
        if high != low and high < count:
            route += [(low, high), (high, low)]
    return lax.ppermute(block, axis, route)


def tile_maxima(left, left_valid, right, right_valid, skip_self):
    row_count = left.shape[0]
    stride = min(512, row_count)
    right_index = jnp.arange(right.shape[0], dtype=jnp.int32)
    scores = lax.dot_general(
        left, right, (((1,), (1,)), ((), ())), preferred_element_type=jnp.float32
    )
    allowed = left_valid[:, None] & right_valid[None, :]
    if skip_self:
        left_index = jnp.arange(stride, dtype=jnp.int32)
        allowed = allowed & (left_index[:, None] != right_index[None, :])
    masked = jnp.where(allowed, scores, -jnp.inf)
    row_parts = jnp.max(masked, axis=1)
    column_best = jnp.max(masked, axis=0)
    return (row_parts, column_best)


def body(embeddings, block_ids):
    row_count, width = embeddings.shape
    devices = lax.axis_size("dev")
    slots = 2 * row_count
    capacity = slots // devices
    values = embeddings.astype(jnp.float32)
    unit_rows = (
        values * lax.rsqrt(jnp.sum(values * values, axis=1, keepdims=True) + 1e-06)
    ).astype(jnp.bfloat16)
    onehot = (block_ids[:, None] == jnp.arange(devices, dtype=jnp.int32)[None, :]).astype(jnp.int32)
    row_rank = jnp.sum(jnp.cumsum(onehot, axis=0) * onehot, axis=1) - 1
    slot_index = block_ids * capacity + row_rank
    outgoing = jnp.zeros((devices * capacity, width), jnp.bfloat16).at[slot_index].set(unit_rows)
    incoming = lax.all_to_all(
        outgoing.reshape(devices, capacity, width), "dev", split_axis=0, concat_axis=0, tiled=True
    )
    own_rows = incoming.reshape(slots, width)
    partner = from_partner(own_rows, "dev", 0)
    own_valid = jnp.any(own_rows != 0, axis=1)
    partner_valid = jnp.any(partner != 0, axis=1)
    parity = lax.axis_index("dev") % 2
    self_best, ignored = tile_maxima(own_rows, own_valid, own_rows, own_valid, True)
    half_rows = slots // 2
    row_parts = []
    column_side = jnp.full((slots,), -jnp.inf, jnp.float32)
    for segment in range(2):
        other_start = (segment ^ parity) * half_rows
        right_rows = lax.dynamic_slice_in_dim(partner, other_start, half_rows, 0)
        right_valid = lax.dynamic_slice_in_dim(partner_valid, other_start, half_rows, 0)
        lower = segment * half_rows
        row_max, column_max = tile_maxima(
            own_rows[lower : lower + half_rows],
            own_valid[lower : lower + half_rows],
            right_rows,
            right_valid,
            False,
        )
        row_parts.append(row_max)
        previous = lax.dynamic_slice_in_dim(column_side, other_start, half_rows, 0)
        column_side = lax.dynamic_update_slice_in_dim(
            column_side, jnp.maximum(previous, column_max), other_start, 0
        )
    returned = from_partner(column_side, "dev", 0)
    cross_best = jnp.maximum(jnp.concatenate(row_parts), returned)
    combined = jnp.where(own_valid, jnp.maximum(self_best, cross_best), 0.0)
    returned_all = lax.all_to_all(
        combined.reshape(devices, capacity), "dev", split_axis=0, concat_axis=0, tiled=True
    )
    return returned_all.reshape(slots)[slot_index]


def solution(mesh):
    placed = (P(("grp", "dev"), None), P(("grp", "dev")))
    return jax.shard_map(
        body, mesh=mesh, in_specs=placed, out_specs=P(("grp", "dev")), check_vma=False
    )
```

profile of v0, /device:TPU:1, one launch (start us, length us, event | category | flops | bytes accessed | tf_op | source)
XLA Modules:
  0.0 105.7 jit_solution(668794776120299973)
XLA Ops:
  0.0 1.2 %fusion.2 = f32[256]{0:T(256)S(1)} fusion(bf16[256,768]{1,0:T(8,128)(2,1)} %param.2), kind=kLoop, calls=%fused_computation.10 | loop fusion | flops 589568 | bytes 394240 | tf_op jit(solution)/shard_map/reduce_sum | solution.py:41
  1.2 0.0 copy-start.1
  1.2 0.7 copy-done.1
  1.8 0.1 copy.5
  2.0 0.0 copy-start
  2.0 0.2 fusion.16
  2.3 0.2 fusion.17
  2.5 0.5 copy-done
  3.0 2.0 %scatter_custom_fusion = bf16[512,768]{1,0:T(8,128)(2,1)S(1)} fusion(s32[256]{0:T(256)S(1)} %compare_select_fusion, bf16[256,768]{1,0:T(8,128)(2,1)S(1)} %copy-done, f32[256]{0:T(256)S(1)} %add_rsqrt_fusion, bf16[]{:T(256)} %constant.13.clone.1), kind=kCustom, calls=%fused_computation.12 | custom fusion | flops 589824 | bytes 1180674 | tf_op jit(solution)/shard_map/scatter | solution.py:46
  4.9 0.2 reshape.52
  5.1 61.6 %all_to_all.14 = bf16[128,4,768]{2,1,0:T(4,128)(2,1)S(1)} all-to-all(bf16[128,4,768]{2,1,0:T(4,128)(2,1)S(1)} %reshape.52), channel_id=1, replica_groups=mesh['grp'=4,'dev'=128] {'dev'}, dimensions={0} | all-to-all | bytes 1572864 | tf_op jit(solution)/shard_map/all_to_all | solution.py:47
  66.7 0.2 reshape.53
  66.9 3.7 %collective-permute-start = (bf16[512,768]{1,0:T(8,128)(2,1)S(1)}, bf16[512,768]{1,0:T(8,128)(2,1)S(1)}, u32[]{:S(2)}, u32[]{:S(2)}) collective-permute-start(bf16[512,768]{1,0:T(8,128)(2,1)S(1)} %reshape.53), channel_id=1, source_target_pairs={{0,1},{1,0},{2,3},{3,2},{4,5},{5,4},{6,7},{7,6},{8,9},{9,8},{10,11... | collective-permute-start | bytes 2359304 | tf_op jit(solution)/shard_map/ppermute | solution.py:14
  70.6 2.3 %compare_reduce_fusion.1 = pred[128,4]{1,0:T(8,128)(4,1)S(1)} fusion(bf16[128,4,768]{2,1,0:T(4,128)(2,1)S(1)} %all_to_all.14), kind=kLoop, calls=%fused_computation.3 | loop fusion | flops 785920 | bytes 786944 | tf_op jit(solution)/shard_map/reduce_or | solution.py:52
  72.9 0.1 reduce_or.21
  73.0 0.1 and.61
  73.1 0.1 and.56
  73.3 0.3 fusion.24
  73.5 0.1 slice.33
  73.6 0.1 slice.30
  73.7 0.0 collective-permute-done
  73.7 0.3 compare_reduce_fusion
  74.0 0.1 fusion.26
  74.1 0.4 fusion.13
  74.5 0.2 dynamic_update_slice.6
  74.7 0.4 fusion.15
  75.1 0.2 maximum_dynamic-update-slice_fusion
  75.3 1.9 %collective-permute-start.1 = (f32[512]{0:T(512)S(1)}, f32[512]{0:T(512)S(1)}, u32[]{:S(2)}, u32[]{:S(2)}) collective-permute-start(f32[512]{0:T(512)S(1)} %maximum_dynamic-update-slice_fusion), channel_id=1, source_target_pairs={{0,1},{1,0},{2,3},{3,2},{4,5},{5,4},{6,7},{7,6},{8,9},{9,8},{10,11... | collective-permute-start | bytes 6152 | tf_op jit(solution)/shard_map/ppermute | solution.py:14
  77.2 0.7 fusion
  77.9 0.5 collective-permute-done.1
  78.3 0.7 all_to_all.10
  79.1 7.9 %all-to-all-start.1 = ((f32[128,1,4]{2,1,0:T(1,128)}), f32[128,1,4]{2,1,0:T(1,128)S(1)}, u32[]{:S(2)}, u32[]{:S(2)}) async-start(f32[128,1,4]{2,1,0:T(1,128)} %bitcast.4), calls=%async_computation.1 | async-start | bytes 131072 | tf_op jit(solution)/shard_map/all_to_all | solution.py:79
  87.0 14.8 %all-to-all-done.1 = f32[128,1,4]{2,1,0:T(1,128)S(1)} async-done(((f32[128,1,4]{2,1,0:T(1,128)}), f32[128,1,4]{2,1,0:T(1,128)S(1)}, u32[]{:S(2)}, u32[]{:S(2)}) %all-to-all-start.1) | async-done | bytes 2080 | tf_op jit(solution)/shard_map/all_to_all | solution.py:79
  101.8 0.5 broadcast.61
  102.3 0.8 reduce.4
  103.1 0.1 reshape.54
  103.2 2.5 %gather_fusion = f32[256]{0:T(256)} fusion(f32[512]{0:T(512)S(1)} %reshape.54, s32[1024]{0:T(1024)S(1)} %pad_clamp_fusion), kind=kCustom, calls=%fused_computation | custom fusion | bytes 3072 | tf_op jit(solution)/shard_map/gather | solution.py:82
  (12 shorter events, 0.1 us)
Async XLA Ops:
  1.2 0.7 copy-start.1
  2.0 1.0 copy-start
  66.9 6.8 %collective-permute-start = (bf16[512,768]{1,0:T(8,128)(2,1)S(1)}, bf16[512,768]{1,0:T(8,128)(2,1)S(1)}, u32[]{:S(2)}, u32[]{:S(2)}) collective-permute-start(bf16[512,768]{1,0:T(8,128)(2,1)S(1)} %reshape.53), channel_id=1, source_target_pairs={{0,1},{1,0},{2,3},{3,2},{4,5},{5,4},{6,7},{7,6},{8,9},{9,8},{10,11... | collective-permute-start | bytes 2359304 | tf_op jit(solution)/shard_map/ppermute | solution.py:14
  75.3 3.0 %collective-permute-start.1 = (f32[512]{0:T(512)S(1)}, f32[512]{0:T(512)S(1)}, u32[]{:S(2)}, u32[]{:S(2)}) collective-permute-start(f32[512]{0:T(512)S(1)} %maximum_dynamic-update-slice_fusion), channel_id=1, source_target_pairs={{0,1},{1,0},{2,3},{3,2},{4,5},{5,4},{6,7},{7,6},{8,9},{9,8},{10,11... | collective-permute-start | bytes 6152 | tf_op jit(solution)/shard_map/ppermute | solution.py:14
  79.1 22.7 %all-to-all-start.1 = ((f32[128,1,4]{2,1,0:T(1,128)}), f32[128,1,4]{2,1,0:T(1,128)S(1)}, u32[]{:S(2)}, u32[]{:S(2)}) async-start(f32[128,1,4]{2,1,0:T(1,128)} %bitcast.4), calls=%async_computation.1 | async-start | bytes 131072 | tf_op jit(solution)/shard_map/all_to_all | solution.py:79
where the time goes:
time: 106 us
  blocking collectives  61.6 us (58%)
  waiting for transfers between devices  15.3 us (14%)
  starting transfers between devices  13.5 us (13%)
  other arithmetic  7.08 us (7%)
  local copies, waits for them, and re-layouts  6.66 us (6%)
  matrix products  1.44 us (1%)
    all_to_all x1, blocking collectives, body(): lax.all_to_all(outgoing.reshape(devices, capacity, width), 'dev', split_a...  61.6 us
    all_to_all x1, waiting for transfers between devices, body(): lax.all_to_all(combined.reshape(devices, capacity), 'dev', split_axis=0,...  14.8 us
    all_to_all x1, starting transfers between devices, body(): lax.all_to_all(combined.reshape(devices, capacity), 'dev', split_axis=0,...  7.88 us
    ppermute x2, starting transfers between devices, from_partner(): return lax.ppermute(block, axis, route)  5.59 us
    gather x1, local copies, waits for them, and re-layouts, body(): return returned_all.reshape(slots)[slot_index]  2.51 us
    reduce_or x1, other arithmetic, body(): own_valid = jnp.any(own_rows != 0, axis=1)  2.27 us
  transfers between devices with their start and end apart: 3, of which 2 were waited for; matrix products, arithmetic and copies ran while one was open for 4% of the time, Pallas kernels for 0%

commit v1 on v0

v1 whole, which is shorter than its diff:
```python
import functools

import jax
import jax.numpy as jnp
from jax import lax
from jax.experimental import pallas as pl
from jax.experimental.pallas import tpu as pltpu
from jax.sharding import PartitionSpec as P

CAPACITY = 8
LANES = 128
LOWEST = -1e30
VMEM_BYTES = 16 * 1024 * 1024


def iota(shape, axis):
    return lax.broadcasted_iota(jnp.int32, shape, axis)


def place_kernel(ids_ref, rows_ref, placed_ref, slot_ref):
    count = rows_ref.shape[0]
    slots = placed_ref.shape[0]
    cluster = jnp.broadcast_to(ids_ref[...] // 2, (count, count))
    above, here = iota((count, count), 0), iota((count, count), 1)
    cluster_above = jnp.sum(jnp.where(above == here, cluster, 0), axis=1, keepdims=True)
    earlier = (cluster_above == cluster) & (above < here)
    rank = jnp.sum(earlier.astype(jnp.int32), axis=0, keepdims=True)
    slot = cluster[:1] * CAPACITY + rank
    slot_ref[...] = slot
    values = rows_ref[...].astype(jnp.float32)
    norm = lax.rsqrt(jnp.sum(values * values, axis=1, keepdims=True) + 1e-06)
    unit = (values * norm).astype(jnp.bfloat16)
    onehot = (iota((slots, count), 0) == slot).astype(jnp.float32).astype(jnp.bfloat16)
    placed_ref[...] = jnp.dot(onehot, unit, preferred_element_type=jnp.float32).astype(
        jnp.bfloat16
    )


def present(rows):
    return jnp.max(jnp.abs(rows).astype(jnp.float32), axis=1, keepdims=True) > 0


def scores_of(others, own):
    return lax.dot_general(
        others, own, (((1,), (1,)), ((), ())), preferred_element_type=jnp.float32
    )


def own_kernel(own_ref, best_ref):
    own = own_ref[...]
    scores = scores_of(own, own)
    allowed = present(own) & (iota(scores.shape, 0) != iota(scores.shape, 1))
    best_ref[...] = jnp.max(jnp.where(allowed, scores, LOWEST), axis=0, keepdims=True)


def cross_kernel(own_ref, other_ref, best_ref, message_ref):
    own, other = own_ref[...], other_ref[...]
    scores = jnp.where(present(other), scores_of(other, own), LOWEST)
    best = jnp.maximum(best_ref[...], jnp.max(scores, axis=0, keepdims=True))
    shape = message_ref.shape
    source, lane = iota(shape, 0), iota(shape, 1)
    message = jnp.zeros(shape, jnp.float32)
    per_part = LANES // CAPACITY
    for part in range(best.shape[1] // LANES):
        mine = source == part * per_part + lane // CAPACITY
        message = jnp.where(mine, best[:, part * LANES : (part + 1) * LANES], message)
    message_ref[...] = message


def pick_kernel(slot_ref, answers_ref, out_ref):
    slot = slot_ref[...]
    answers = answers_ref[...]
    count = slot.shape[1]
    onehot = (iota((answers.shape[0], count), 0) == slot // CAPACITY).astype(jnp.float32)
    found = lax.dot_general(
        answers,
        onehot,
        (((0,), (0,)), ((), ())),
        precision=lax.Precision.HIGHEST,
        preferred_element_type=jnp.float32,
    )
    mine = iota(found.shape, 0) % CAPACITY == slot % CAPACITY
    out_ref[...] = jnp.sum(jnp.where(mine, found, 0.0), axis=0, keepdims=True)


def call(kernel, outs, flops, *args):
    whole = pl.BlockSpec(memory_space=pltpu.VMEM)
    moved = sum(a.size * a.dtype.itemsize for a in args)
    return pl.pallas_call(
        kernel,
        out_shape=outs,
        in_specs=[whole] * len(args),
        out_specs=jax.tree.map(lambda _: whole, outs),
        compiler_params=pltpu.CompilerParams(vmem_limit_bytes=VMEM_BYTES),
        cost_estimate=pl.CostEstimate(flops=flops, bytes_accessed=moved, transcendentals=0),
    )(*args)


def body(embeddings, block_ids):
    count, width = embeddings.shape
    devices = lax.axis_size("dev")
    chips = devices // 2
    slots = chips * CAPACITY
    same_core = [[2 * chip + core for chip in range(chips)] for core in range(2)]
    exchange = functools.partial(
        lax.all_to_all,
        axis_name="dev",
        split_axis=0,
        concat_axis=0,
        axis_index_groups=same_core,
        tiled=True,
    )
    row = jax.ShapeDtypeStruct
    placed, slot = call(
        place_kernel,
        (row((slots, width), jnp.bfloat16), row((1, count), jnp.int32)),
        2 * slots * count * width,
        block_ids.reshape(1, count),
        embeddings,
    )
    own = exchange(placed.reshape(chips, CAPACITY, width)).reshape(slots, width)
    other = lax.ppermute(own, "dev", [(d, d ^ 1) for d in range(devices)])
    flops = 2 * slots * slots * width
    best = call(own_kernel, row((1, slots), jnp.float32), flops, own)
    message = call(cross_kernel, row((chips, LANES), jnp.float32), flops, own, other, best)
    answers = exchange(message.reshape(chips, 1, LANES)).reshape(chips, LANES)
    out = call(pick_kernel, row((1, count), jnp.float32), 2 * chips * LANES * count, slot, answers)
    return out.reshape(count)


def solution(mesh):
    placed = (P(("grp", "dev"), None), P(("grp", "dev")))
    return jax.shard_map(
        body, mesh=mesh, in_specs=placed, out_specs=P(("grp", "dev")), check_vma=False
    )
```

time: 106 us -> 90.8 us (0.86)
  blocking collectives: 61.6 us -> 78.4 us
  waiting for transfers between devices: 15.3 us -> 1.26 us
  starting transfers between devices: 13.5 us -> 6.24 us
  other arithmetic: 7.08 us -> 0 us
  local copies, waits for them, and re-layouts: 6.66 us -> 1.67 us
  Pallas kernels: 0 us -> 2.69 us
  matrix products: 1.44 us -> 0 us
    all_to_all x1 -> x2, blocking collectives: 61.6 us -> 78.4 us  [the longest x1 59.6 us: body(): own = exchange(placed.reshape(chips, CAPACITY, width)).reshape(slots, width)]
    all_to_all x1 -> x0, waiting for transfers between devices: 14.8 us -> none  [body(): lax.all_to_all(combined.reshape(devices, capacity), 'dev', split_axis=0,...]
    all_to_all x1 -> x0, starting transfers between devices: 7.88 us -> none  [body(): lax.all_to_all(combined.reshape(devices, capacity), 'dev', split_axis=0,...]
    pallas_call x0 -> x4, Pallas kernels: none -> 2.69 us  [call(): pl.pallas_call(kernel, out_shape=outs, in_specs=[whole] * len(args), out_...]
    reduce_or x2 -> x0, other arithmetic: 2.53 us -> none  [the longest x1 2.27 us: body(): own_valid = jnp.any(own_rows != 0, axis=1)]
    gather x1 -> x0, local copies, waits for them, and re-layouts: 2.51 us -> none  [body(): return returned_all.reshape(slots)[slot_index]]
    scatter x1 -> x0, other arithmetic: 1.97 us -> none  [body(): jnp.zeros((devices * capacity, width), jnp.bfloat16).at[slot_index]]
    dot_general x3 -> x0, matrix products: 1.44 us -> none  [tile_maxima(): lax.dot_general(left, right, (((1,), (1,)), ((), ())), preferred_element_...]
  transfers between devices with their start and end apart: 3 -> 1, of which waited for: 2 -> 1; matrix products, arithmetic and copies ran while one was open for 4% -> 0% of each run, Pallas kernels for 0% -> 1%
where the time goes in v1:
time: 90.8 us; the launch traced here: 90.3 us
  blocking collectives  78.4 us (86%)
  starting transfers between devices  6.24 us (7%)
  Pallas kernels  2.69 us (3%)
  local copies, waits for them, and re-layouts  1.67 us (2%)
  waiting for transfers between devices  1.26 us (1%)
    all_to_all x1, blocking collectives, body(): own = exchange(placed.reshape(chips, CAPACITY, width)).reshape(slots, width)  59.6 us
    all_to_all x1, blocking collectives, body(): answers = exchange(message.reshape(chips, 1, LANES)).reshape(chips, LANES)  18.8 us
    ppermute x1, starting transfers between devices, body(): other = lax.ppermute(own, 'dev', [(d, d ^ 1) for d in range(devices)])  6.24 us
    pallas_call x4, Pallas kernels, call(): pl.pallas_call(kernel, out_shape=outs, in_specs=[whole] * len(args), out_...  2.69 us
  transfers between devices with their start and end apart: 1, of which 1 were waited for; matrix products, arithmetic and copies ran while one was open for 0% of the time, Pallas kernels for 1%

profile of v1, /device:TPU:1, one launch (start us, length us, event | category | flops | bytes accessed | tf_op | source)
XLA Modules:
  0.0 90.3 jit_solution(14103458592613106256)
XLA Ops:
  0.0 0.0 copy-start.1
  0.0 0.7 copy-done.1
  0.7 0.0 copy-start
  0.7 1.0 %copy-done = bf16[256,768]{1,0:T(8,128)(2,1)S(1)} copy-done((bf16[256,768]{1,0:T(8,128)(2,1)S(1)}, bf16[256,768]{1,0:T(8,128)(2,1)}, u32[]{:S(2)}) %copy-start) | copy-done | bytes 393240
  1.7 0.6 shard_map.28
  2.2 59.6 %all_to_all.10 = bf16[64,8,768]{2,1,0:T(8,128)(2,1)S(1)} all-to-all(bf16[64,8,768]{2,1,0:T(8,128)(2,1)S(1)} %bitcast.11), channel_id=1, replica_groups={{0,2,4,6,8,10,12,14,16,18,20,22,24,26,28,30,32,34,36,38,40,42,44,46,48,..., dimensions={0} | all-to-all | bytes 1572864 | tf_op jit(solution)/shard_map/all_to_all | solution.py:121
  61.8 6.2 %collective-permute-start = (bf16[512,768]{1,0:T(8,128)(2,1)S(1)}, bf16[512,768]{1,0:T(8,128)(2,1)S(1)}, u32[]{:S(2)}, u32[]{:S(2)}) collective-permute-start(bf16[512,768]{1,0:T(8,128)(2,1)S(1)} %bitcast.8), channel_id=1, source_target_pairs={{0,1},{1,0},{2,3},{3,2},{4,5},{5,4},{6,7},{7,6},{8,9},{9,8},{10,11... | collective-permute-start | bytes 2359304 | tf_op jit(solution)/shard_map/ppermute | solution.py:122
  68.1 0.6 shard_map.29.best_ref
  68.7 1.3 %collective-permute-done.other_ref = bf16[512,768]{1,0:T(8,128)(2,1)S(1)} collective-permute-done((bf16[512,768]{1,0:T(8,128)(2,1)S(1)}, bf16[512,768]{1,0:T(8,128)(2,1)S(1)}, u32[]{:S(2)}, u32[]{:S(2)}) %collective-permute-start) | collective-permute-done | bytes 786464 | tf_op jit(solution)/shard_map/ppermute | solution.py:122
  69.9 0.6 shard_map.30
  70.6 18.8 %all_to_all.11 = f32[64,1,128]{2,1,0:T(1,128)S(1)} all-to-all(f32[64,1,128]{2,1,0:T(1,128)S(1)} %bitcast.12), channel_id=1, replica_groups={{0,2,4,6,8,10,12,14,16,18,20,22,24,26,28,30,32,34,36,38,40,42,44,46,48,..., dimensions={0} | all-to-all | bytes 65536 | tf_op jit(solution)/shard_map/all_to_all | solution.py:126
  89.4 0.9 shard_map.31
Async XLA Ops:
  0.0 0.7 copy-start.1
  0.7 1.0 %copy-start = (bf16[256,768]{1,0:T(8,128)(2,1)S(1)}, bf16[256,768]{1,0:T(8,128)(2,1)}, u32[]{:S(2)}) copy-start(bf16[256,768]{1,0:T(8,128)(2,1)} %rows_ref.1) | copy-start | bytes 1179652
  61.8 8.1 %collective-permute-start = (bf16[512,768]{1,0:T(8,128)(2,1)S(1)}, bf16[512,768]{1,0:T(8,128)(2,1)S(1)}, u32[]{:S(2)}, u32[]{:S(2)}) collective-permute-start(bf16[512,768]{1,0:T(8,128)(2,1)S(1)} %bitcast.8), channel_id=1, source_target_pairs={{0,1},{1,0},{2,3},{3,2},{4,5},{5,4},{6,7},{7,6},{8,9},{9,8},{10,11... | collective-permute-start | bytes 2359304 | tf_op jit(solution)/shard_map/ppermute | solution.py:122

commit v2 on v1

v2 whole, which is shorter than its diff:
```python
import functools

import jax
import jax.numpy as jnp
from jax import lax
from jax.experimental import pallas as pl
from jax.experimental.pallas import tpu as pltpu
from jax.sharding import PartitionSpec as P

CAPACITY = 8
LANES = 128
LOWEST = -1e30
ROWS_FIRST = 42
ANSWERS_FIRST = 34
SLOT_COST = 2_000_000_000
VMEM_BYTES = 16 * 1024 * 1024


def iota(shape, axis):
    return lax.broadcasted_iota(jnp.int32, shape, axis)


def slot_kernel(ids_ref, slot_ref):
    count = ids_ref.shape[1]
    cluster = jnp.broadcast_to(ids_ref[...] // 2, (count, count))
    above, here = iota((count, count), 0), iota((count, count), 1)
    cluster_above = jnp.sum(jnp.where(above == here, cluster, 0), axis=1, keepdims=True)
    earlier = (cluster_above == cluster) & (above < here)
    rank = jnp.sum(earlier.astype(jnp.int32), axis=0, keepdims=True)
    slot_ref[...] = cluster[:1] * CAPACITY + rank


def place_kernel(slot_ref, rows_ref, placed_ref):
    values = rows_ref[...].astype(jnp.float32)
    norm = lax.rsqrt(jnp.sum(values * values, axis=1, keepdims=True) + 1e-06)
    unit = (values * norm).astype(jnp.bfloat16)
    shape = (placed_ref.shape[0], rows_ref.shape[0])
    onehot = (iota(shape, 0) == slot_ref[...]).astype(jnp.float32).astype(jnp.bfloat16)
    placed_ref[...] = jnp.dot(onehot, unit, preferred_element_type=jnp.float32).astype(
        jnp.bfloat16
    )


def present(rows):
    return jnp.max(jnp.abs(rows).astype(jnp.float32), axis=1, keepdims=True) > 0


def scores_of(others, own):
    return lax.dot_general(
        others, own, (((1,), (1,)), ((), ())), preferred_element_type=jnp.float32
    )


def own_kernel(own_ref, best_ref):
    own = own_ref[...]
    scores = scores_of(own, own)
    allowed = present(own) & (iota(scores.shape, 0) != iota(scores.shape, 1))
    best_ref[...] = jnp.max(jnp.where(allowed, scores, LOWEST), axis=0, keepdims=True)


def turned(place, turn, chips):
    place = place + turn
    return jnp.where(place < chips, place, place - chips)


def cross_kernel(turn, own_ref, other_ref, best_ref, message_ref):
    own, other = own_ref[...], other_ref[...]
    scores = jnp.where(present(other), scores_of(other, own), LOWEST)
    best = jnp.maximum(best_ref[...], jnp.max(scores, axis=0, keepdims=True))
    shape = message_ref.shape
    source, lane = turned(iota(shape, 0), turn, shape[0]), iota(shape, 1)
    message = jnp.zeros(shape, jnp.float32)
    per_part = LANES // CAPACITY
    for part in range(best.shape[1] // LANES):
        mine = source == part * per_part + lane // CAPACITY
        message = jnp.where(mine, best[:, part * LANES : (part + 1) * LANES], message)
    message_ref[...] = message


def pick_kernel(turn, slot_ref, answers_ref, out_ref):
    slot = slot_ref[...]
    answers = answers_ref[...]
    count = slot.shape[1]
    chips = answers.shape[0]
    cluster = turned(iota((chips, count), 0), turn, chips)
    onehot = (cluster == slot // CAPACITY).astype(jnp.float32).astype(jnp.bfloat16)
    parts = []
    for _ in range(3):
        parts.append(answers.astype(jnp.bfloat16))
        answers = answers - parts[-1].astype(jnp.float32)
    found = lax.dot_general(
        jnp.concatenate(parts, axis=0),
        jnp.concatenate([onehot] * 3, axis=0),
        (((0,), (0,)), ((), ())),
        preferred_element_type=jnp.float32,
    )
    mine = iota(found.shape, 0) % CAPACITY == slot % CAPACITY
    out_ref[...] = jnp.sum(jnp.where(mine, found, 0.0), axis=0, keepdims=True)


def groups(first, chips):
    return [[2 * ((first + k) % chips) + core for k in range(chips)] for core in range(2)]


def call(kernel, outs, flops, *args):
    whole = pl.BlockSpec(memory_space=pltpu.VMEM)
    moved = sum(a.size * a.dtype.itemsize for a in args)
    return pl.pallas_call(
        kernel,
        out_shape=outs,
        in_specs=[whole] * len(args),
        out_specs=jax.tree.map(lambda _: whole, outs),
        compiler_params=pltpu.CompilerParams(vmem_limit_bytes=VMEM_BYTES),
        cost_estimate=pl.CostEstimate(flops=flops, bytes_accessed=moved, transcendentals=0),
    )(*args)


def body(embeddings, block_ids):
    count, width = embeddings.shape
    devices = lax.axis_size("dev")
    chips = devices // 2
    slots = chips * CAPACITY
    turn = (ANSWERS_FIRST - ROWS_FIRST) % chips

    def exchange(blocks, first):
        return lax.all_to_all(
            blocks, "dev", 0, 0, axis_index_groups=groups(first, chips), tiled=True
        )

    row = jax.ShapeDtypeStruct
    slot = call(
        slot_kernel, row((1, count), jnp.int32), SLOT_COST, block_ids.reshape(1, count)
    )
    placed = call(
        place_kernel,
        row((slots, width), jnp.bfloat16),
        2 * slots * count * width,
        slot,
        embeddings,
    )
    own = exchange(placed.reshape(chips, CAPACITY, width), ROWS_FIRST).reshape(slots, width)
    other = lax.ppermute(own, "dev", [(d, d ^ 1) for d in range(devices)])
    flops = 2 * slots * slots * width
    best = call(own_kernel, row((1, slots), jnp.float32), flops, own)
    cross = functools.partial(cross_kernel, turn)
    message = call(cross, row((chips, LANES), jnp.float32), flops, own, other, best)
    answers = exchange(message.reshape(chips, 1, LANES), ANSWERS_FIRST)
    answers = answers.reshape(chips, LANES)
    flops = 6 * chips * LANES * count
    pick = functools.partial(pick_kernel, turn)
    out = call(pick, row((1, count), jnp.float32), flops, slot, answers)
    return out.reshape(count)


def solution(mesh):
    placed = (P(("grp", "dev"), None), P(("grp", "dev")))
    return jax.shard_map(
        body, mesh=mesh, in_specs=placed, out_specs=P(("grp", "dev")), check_vma=False
    )
```

time: 90.8 us -> 82.2 us (0.905)
  blocking collectives: 78.4 us -> 71.1 us
  starting transfers between devices: 6.24 us -> 5.12 us
    all_to_all x2, blocking collectives: 78.4 us -> 71.1 us  [exchange(): lax.all_to_all(blocks, 'dev', 0, 0, axis_index_groups=groups(first, chips...]
    ppermute x1, starting transfers between devices: 6.24 us -> 5.12 us  [body(): other = lax.ppermute(own, 'dev', [(d, d ^ 1) for d in range(devices)])]
    pallas_call x4 -> x5, Pallas kernels: 2.69 us -> 2.68 us  [call(): pl.pallas_call(kernel, out_shape=outs, in_specs=[whole] * len(args), out_...]
where the time goes in v2:
time: 82.2 us; the launch traced here: 81.7 us
  blocking collectives  71.1 us (86%)
  starting transfers between devices  5.12 us (6%)
  Pallas kernels  2.68 us (3%)
  local copies, waits for them, and re-layouts  1.51 us (2%)
  waiting for transfers between devices  1.27 us (2%)
    all_to_all x2, blocking collectives, exchange(): lax.all_to_all(blocks, 'dev', 0, 0, axis_index_groups=groups(first, chips...  71.1 us
    ppermute x1, starting transfers between devices, body(): other = lax.ppermute(own, 'dev', [(d, d ^ 1) for d in range(devices)])  5.12 us
    pallas_call x5, Pallas kernels, call(): pl.pallas_call(kernel, out_shape=outs, in_specs=[whole] * len(args), out_...  2.68 us
  transfers between devices with their start and end apart: 1, of which 1 were waited for; matrix products, arithmetic and copies ran while one was open for 0% of the time, Pallas kernels for 1%

profile of v2, /device:TPU:1, one launch (start us, length us, event | category | flops | bytes accessed | tf_op | source)
XLA Modules:
  0.0 81.7 jit_solution(8060238499538358969)
XLA Ops:
  0.0 0.0 copy-start.1
  0.0 0.7 copy-done.1
  0.7 0.0 copy-start
  0.7 0.2 shard_map.28.slot_ref
  0.8 0.8 %copy-done = bf16[256,768]{1,0:T(8,128)(2,1)S(1)} copy-done((bf16[256,768]{1,0:T(8,128)(2,1)S(1)}, bf16[256,768]{1,0:T(8,128)(2,1)}, u32[]{:S(2)}) %copy-start) | copy-done | bytes 393240
  1.7 0.5 shard_map.29
  2.2 54.1 %all_to_all.10 = bf16[64,8,768]{2,1,0:T(8,128)(2,1)S(1)} all-to-all(bf16[64,8,768]{2,1,0:T(8,128)(2,1)S(1)} %bitcast.11), channel_id=1, replica_groups={{84,86,88,90,92,94,96,98,100,102,104,106,108,110,112,114,116,118,120,12..., dimensions={0} | all-to-all | bytes 1572864 | tf_op jit(solution)/shard_map/all_to_all | solution.py:126
  56.3 5.1 %collective-permute-start = (bf16[512,768]{1,0:T(8,128)(2,1)S(1)}, bf16[512,768]{1,0:T(8,128)(2,1)S(1)}, u32[]{:S(2)}, u32[]{:S(2)}) collective-permute-start(bf16[512,768]{1,0:T(8,128)(2,1)S(1)} %bitcast.8), channel_id=1, source_target_pairs={{0,1},{1,0},{2,3},{3,2},{4,5},{5,4},{6,7},{7,6},{8,9},{9,8},{10,11... | collective-permute-start | bytes 2359304 | tf_op jit(solution)/shard_map/ppermute | solution.py:142
  61.4 0.6 shard_map.30.best_ref
  62.0 1.3 %collective-permute-done.other_ref = bf16[512,768]{1,0:T(8,128)(2,1)S(1)} collective-permute-done((bf16[512,768]{1,0:T(8,128)(2,1)S(1)}, bf16[512,768]{1,0:T(8,128)(2,1)S(1)}, u32[]{:S(2)}, u32[]{:S(2)}) %collective-permute-start) | collective-permute-done | bytes 786464 | tf_op jit(solution)/shard_map/ppermute | solution.py:142
  63.3 0.6 shard_map.31
  63.9 17.0 %all_to_all.11 = f32[64,1,128]{2,1,0:T(1,128)S(1)} all-to-all(f32[64,1,128]{2,1,0:T(1,128)S(1)} %bitcast.12), channel_id=1, replica_groups={{68,70,72,74,76,78,80,82,84,86,88,90,92,94,96,98,100,102,104,106,108,11..., dimensions={0} | all-to-all | bytes 65536 | tf_op jit(solution)/shard_map/all_to_all | solution.py:126
  80.9 0.8 shard_map.32
Async XLA Ops:
  0.0 0.7 copy-start.1
  0.7 1.0 %copy-start = (bf16[256,768]{1,0:T(8,128)(2,1)S(1)}, bf16[256,768]{1,0:T(8,128)(2,1)}, u32[]{:S(2)}) copy-start(bf16[256,768]{1,0:T(8,128)(2,1)} %rows_ref.1) | copy-start | bytes 1179652
  56.3 7.0 %collective-permute-start = (bf16[512,768]{1,0:T(8,128)(2,1)S(1)}, bf16[512,768]{1,0:T(8,128)(2,1)S(1)}, u32[]{:S(2)}, u32[]{:S(2)}) collective-permute-start(bf16[512,768]{1,0:T(8,128)(2,1)S(1)} %bitcast.8), channel_id=1, source_target_pairs={{0,1},{1,0},{2,3},{3,2},{4,5},{5,4},{6,7},{7,6},{8,9},{9,8},{10,11... | collective-permute-start | bytes 2359304 | tf_op jit(solution)/shard_map/ppermute | solution.py:142

commit v3 on v2

--- a/solution.py
+++ b/solution.py
@@ -12,7 +12,8 @@
 LOWEST = -1e30
 ROWS_FIRST = 42
 ANSWERS_FIRST = 34
-SLOT_COST = 2_000_000_000
+ORDER_COST = 10_000_000_000
+SLOT_COST = 1_000_000
 VMEM_BYTES = 16 * 1024 * 1024
 
 
@@ -20,13 +21,17 @@
     return lax.broadcasted_iota(jnp.int32, shape, axis)
 
 
-def slot_kernel(ids_ref, slot_ref):
-    count = ids_ref.shape[1]
-    cluster = jnp.broadcast_to(ids_ref[...] // 2, (count, count))
-    above, here = iota((count, count), 0), iota((count, count), 1)
-    cluster_above = jnp.sum(jnp.where(above == here, cluster, 0), axis=1, keepdims=True)
-    earlier = (cluster_above == cluster) & (above < here)
-    rank = jnp.sum(earlier.astype(jnp.int32), axis=0, keepdims=True)
+def order_kernel(same_ref, earlier_ref):
+    above, here = iota(same_ref.shape, 0), iota(same_ref.shape, 1)
+    same_ref[...] = (above == here).astype(jnp.int32)
+    earlier_ref[...] = (above < here).astype(jnp.int32)
+
+
+def slot_kernel(ids_ref, same_ref, earlier_ref, slot_ref):
+    cluster = jnp.broadcast_to(ids_ref[...] // 2, same_ref.shape)
+    cluster_above = jnp.sum(cluster * same_ref[...], axis=1, keepdims=True)
+    earlier = jnp.where(cluster_above == cluster, earlier_ref[...], 0)
+    rank = jnp.sum(earlier, axis=0, keepdims=True)
     slot_ref[...] = cluster[:1] * CAPACITY + rank
 
 
@@ -128,8 +133,10 @@
         )
 
     row = jax.ShapeDtypeStruct
+    square = row((count, count), jnp.int32)
+    masks = call(order_kernel, (square, square), ORDER_COST)
     slot = call(
-        slot_kernel, row((1, count), jnp.int32), SLOT_COST, block_ids.reshape(1, count)
+        slot_kernel, row((1, count), jnp.int32), SLOT_COST, block_ids.reshape(1, count), *masks
     )
     placed = call(
         place_kernel,

time: 82.2 us -> 81.5 us (level)
    pallas_call x5 -> x6, Pallas kernels: 2.68 us -> 2.72 us  [call(): pl.pallas_call(kernel, out_shape=outs, in_specs=[whole] * len(args), out_...]
where the time goes in v3:
time: 81.5 us; the launch traced here: 81 us
  blocking collectives  71.1 us (87%)
  starting transfers between devices  5.12 us (6%)
  Pallas kernels  2.72 us (3%)
  waiting for transfers between devices  1.27 us (2%)
  local copies, waits for them, and re-layouts  0.82 us (1%)
    all_to_all x2, blocking collectives, exchange(): lax.all_to_all(blocks, 'dev', 0, 0, axis_index_groups=groups(first, chips...  71.1 us
    ppermute x1, starting transfers between devices, body(): other = lax.ppermute(own, 'dev', [(d, d ^ 1) for d in range(devices)])  5.12 us
    pallas_call x6, Pallas kernels, call(): pl.pallas_call(kernel, out_shape=outs, in_specs=[whole] * len(args), out_...  2.72 us
  transfers between devices with their start and end apart: 1, of which 1 were waited for; matrix products, arithmetic and copies ran while one was open for 0% of the time, Pallas kernels for 1%

profile of v3, /device:TPU:1, one launch (start us, length us, event | category | flops | bytes accessed | tf_op | source)
XLA Modules:
  0.0 81.0 jit_solution(14375364358668818413)
XLA Ops:
  0.0 0.0 copy-start.1
  0.0 0.0 copy-start
  0.1 0.6 copy-done.1
  0.7 0.2 shard_map.29.slot_ref
  0.8 0.2 copy-done
  1.0 0.5 shard_map.30
  1.5 54.1 %all_to_all.10 = bf16[64,8,768]{2,1,0:T(8,128)(2,1)S(1)} all-to-all(bf16[64,8,768]{2,1,0:T(8,128)(2,1)S(1)} %bitcast.11), channel_id=1, replica_groups={{84,86,88,90,92,94,96,98,100,102,104,106,108,110,112,114,116,118,120,12..., dimensions={0} | all-to-all | bytes 1572864 | tf_op jit(solution)/shard_map/all_to_all | solution.py:131
  55.7 5.1 %collective-permute-start = (bf16[512,768]{1,0:T(8,128)(2,1)S(1)}, bf16[512,768]{1,0:T(8,128)(2,1)S(1)}, u32[]{:S(2)}, u32[]{:S(2)}) collective-permute-start(bf16[512,768]{1,0:T(8,128)(2,1)S(1)} %bitcast.8), channel_id=1, source_target_pairs={{0,1},{1,0},{2,3},{3,2},{4,5},{5,4},{6,7},{7,6},{8,9},{9,8},{10,11... | collective-permute-start | bytes 2359304 | tf_op jit(solution)/shard_map/ppermute | solution.py:149
  60.8 0.6 shard_map.31.best_ref
  61.4 1.3 %collective-permute-done.other_ref = bf16[512,768]{1,0:T(8,128)(2,1)S(1)} collective-permute-done((bf16[512,768]{1,0:T(8,128)(2,1)S(1)}, bf16[512,768]{1,0:T(8,128)(2,1)S(1)}, u32[]{:S(2)}, u32[]{:S(2)}) %collective-permute-start) | collective-permute-done | bytes 786464 | tf_op jit(solution)/shard_map/ppermute | solution.py:149
  62.7 0.6 shard_map.32
  63.3 16.9 %all_to_all.11 = f32[64,1,128]{2,1,0:T(1,128)S(1)} all-to-all(f32[64,1,128]{2,1,0:T(1,128)S(1)} %bitcast.12), channel_id=1, replica_groups={{68,70,72,74,76,78,80,82,84,86,88,90,92,94,96,98,100,102,104,106,108,11..., dimensions={0} | all-to-all | bytes 65536 | tf_op jit(solution)/shard_map/all_to_all | solution.py:131
  80.3 0.8 shard_map.33
  (1 shorter events, 0.0 us)
Async XLA Ops:
  0.0 0.7 copy-start.1
  0.0 1.0 %copy-start = (bf16[256,768]{1,0:T(8,128)(2,1)S(1)}, bf16[256,768]{1,0:T(8,128)(2,1)}, u32[]{:S(2)}) copy-start(bf16[256,768]{1,0:T(8,128)(2,1)} %rows_ref.1) | copy-start | bytes 1179652
  55.7 7.0 %collective-permute-start = (bf16[512,768]{1,0:T(8,128)(2,1)S(1)}, bf16[512,768]{1,0:T(8,128)(2,1)S(1)}, u32[]{:S(2)}, u32[]{:S(2)}) collective-permute-start(bf16[512,768]{1,0:T(8,128)(2,1)S(1)} %bitcast.8), channel_id=1, source_target_pairs={{0,1},{1,0},{2,3},{3,2},{4,5},{5,4},{6,7},{7,6},{8,9},{9,8},{10,11... | collective-permute-start | bytes 2359304 | tf_op jit(solution)/shard_map/ppermute | solution.py:149

commit v4 on v3

--- a/solution.py
+++ b/solution.py
@@ -10,10 +10,9 @@
 CAPACITY = 8
 LANES = 128
 LOWEST = -1e30
-ROWS_FIRST = 42
+ROWS_FIRST = 47
 ANSWERS_FIRST = 34
 ORDER_COST = 10_000_000_000
-SLOT_COST = 1_000_000
 VMEM_BYTES = 16 * 1024 * 1024
 
 
@@ -27,20 +26,18 @@
     earlier_ref[...] = (above < here).astype(jnp.int32)
 
 
-def slot_kernel(ids_ref, same_ref, earlier_ref, slot_ref):
+def place_kernel(ids_ref, same_ref, earlier_ref, rows_ref, placed_ref, slot_ref):
     cluster = jnp.broadcast_to(ids_ref[...] // 2, same_ref.shape)
     cluster_above = jnp.sum(cluster * same_ref[...], axis=1, keepdims=True)
     earlier = jnp.where(cluster_above == cluster, earlier_ref[...], 0)
     rank = jnp.sum(earlier, axis=0, keepdims=True)
-    slot_ref[...] = cluster[:1] * CAPACITY + rank
-
-
-def place_kernel(slot_ref, rows_ref, placed_ref):
+    slot = cluster[:1] * CAPACITY + rank
+    slot_ref[...] = slot
     values = rows_ref[...].astype(jnp.float32)
     norm = lax.rsqrt(jnp.sum(values * values, axis=1, keepdims=True) + 1e-06)
     unit = (values * norm).astype(jnp.bfloat16)
     shape = (placed_ref.shape[0], rows_ref.shape[0])
-    onehot = (iota(shape, 0) == slot_ref[...]).astype(jnp.float32).astype(jnp.bfloat16)
+    onehot = (iota(shape, 0) == slot).astype(jnp.float32).astype(jnp.bfloat16)
     placed_ref[...] = jnp.dot(onehot, unit, preferred_element_type=jnp.float32).astype(
         jnp.bfloat16
     )
@@ -135,14 +132,12 @@
     row = jax.ShapeDtypeStruct
     square = row((count, count), jnp.int32)
     masks = call(order_kernel, (square, square), ORDER_COST)
-    slot = call(
-        slot_kernel, row((1, count), jnp.int32), SLOT_COST, block_ids.reshape(1, count), *masks
-    )
-    placed = call(
+    placed, slot = call(
         place_kernel,
-        row((slots, width), jnp.bfloat16),
+        (row((slots, width), jnp.bfloat16), row((1, count), jnp.int32)),
         2 * slots * count * width,
-        slot,
+        block_ids.reshape(1, count),
+        *masks,
         embeddings,
     )
     own = exchange(placed.reshape(chips, CAPACITY, width), ROWS_FIRST).reshape(slots, width)

time: 81.5 us -> 81.5 us (level)
  starting transfers between devices: 5.12 us -> 3.29 us
  blocking collectives: 71.1 us -> 72.8 us
    ppermute x1, starting transfers between devices: 5.12 us -> 3.29 us  [body(): other = lax.ppermute(own, 'dev', [(d, d ^ 1) for d in range(devices)])]
    all_to_all x2, blocking collectives: 71.1 us -> 72.8 us  [exchange(): lax.all_to_all(blocks, 'dev', 0, 0, axis_index_groups=groups(first, chips...]
    pallas_call x6 -> x5, Pallas kernels: 2.72 us -> 2.61 us  [call(): pl.pallas_call(kernel, out_shape=outs, in_specs=[whole] * len(args), out_...]
where the time goes in v4:
time: 81.5 us; the launch traced here: 81 us
  blocking collectives  72.8 us (89%)
  starting transfers between devices  3.29 us (4%)
  Pallas kernels  2.61 us (3%)
  waiting for transfers between devices  1.27 us (2%)
  local copies, waits for them, and re-layouts  0.95 us (1%)
    all_to_all x2, blocking collectives, exchange(): lax.all_to_all(blocks, 'dev', 0, 0, axis_index_groups=groups(first, chips...  72.8 us
    ppermute x1, starting transfers between devices, body(): other = lax.ppermute(own, 'dev', [(d, d ^ 1) for d in range(devices)])  3.29 us
    pallas_call x5, Pallas kernels, call(): pl.pallas_call(kernel, out_shape=outs, in_specs=[whole] * len(args), out_...  2.61 us
  transfers between devices with their start and end apart: 1, of which 1 were waited for; matrix products, arithmetic and copies ran while one was open for 0% of the time, Pallas kernels for 1%

profile of v4, /device:TPU:1, one launch (start us, length us, event | category | flops | bytes accessed | tf_op | source)
XLA Modules:
  0.0 81.0 jit_solution(15857434397080160174)
XLA Ops:
  0.0 0.0 copy-start
  0.0 0.0 copy-start.1
  0.1 0.9 %copy-done = bf16[256,768]{1,0:T(8,128)(2,1)S(1)} copy-done((bf16[256,768]{1,0:T(8,128)(2,1)S(1)}, bf16[256,768]{1,0:T(8,128)(2,1)}, u32[]{:S(2)}) %copy-start) | copy-done | bytes 393240
  1.0 0.0 copy-done.1
  1.0 0.6 shard_map.29
  1.6 55.3 %all_to_all.10 = bf16[64,8,768]{2,1,0:T(8,128)(2,1)S(1)} all-to-all(bf16[64,8,768]{2,1,0:T(8,128)(2,1)S(1)} %bitcast.11), channel_id=1, replica_groups={{94,96,98,100,102,104,106,108,110,112,114,116,118,120,122,124,126,0,2,4..., dimensions={0} | all-to-all | bytes 1572864 | tf_op jit(solution)/shard_map/all_to_all | solution.py:128
  56.9 3.3 %collective-permute-start = (bf16[512,768]{1,0:T(8,128)(2,1)S(1)}, bf16[512,768]{1,0:T(8,128)(2,1)S(1)}, u32[]{:S(2)}, u32[]{:S(2)}) collective-permute-start(bf16[512,768]{1,0:T(8,128)(2,1)S(1)} %bitcast.8), channel_id=1, source_target_pairs={{0,1},{1,0},{2,3},{3,2},{4,5},{5,4},{6,7},{7,6},{8,9},{9,8},{10,11... | collective-permute-start | bytes 2359304 | tf_op jit(solution)/shard_map/ppermute | solution.py:144
  60.2 0.6 shard_map.30.best_ref
  60.8 1.3 %collective-permute-done.other_ref = bf16[512,768]{1,0:T(8,128)(2,1)S(1)} collective-permute-done((bf16[512,768]{1,0:T(8,128)(2,1)S(1)}, bf16[512,768]{1,0:T(8,128)(2,1)S(1)}, u32[]{:S(2)}, u32[]{:S(2)}) %collective-permute-start) | collective-permute-done | bytes 786464 | tf_op jit(solution)/shard_map/ppermute | solution.py:144
  62.1 0.6 shard_map.31
  62.7 17.5 %all_to_all.11 = f32[64,1,128]{2,1,0:T(1,128)S(1)} all-to-all(f32[64,1,128]{2,1,0:T(1,128)S(1)} %bitcast.12), channel_id=1, replica_groups={{68,70,72,74,76,78,80,82,84,86,88,90,92,94,96,98,100,102,104,106,108,11..., dimensions={0} | all-to-all | bytes 65536 | tf_op jit(solution)/shard_map/all_to_all | solution.py:128
  80.2 0.8 shard_map.32
  (1 shorter events, 0.0 us)
Async XLA Ops:
  0.0 1.0 %copy-start = (bf16[256,768]{1,0:T(8,128)(2,1)S(1)}, bf16[256,768]{1,0:T(8,128)(2,1)}, u32[]{:S(2)}) copy-start(bf16[256,768]{1,0:T(8,128)(2,1)} %rows_ref.1) | copy-start | bytes 1179652
  0.0 1.0 %copy-start.1 = (s32[256]{0:T(256)S(1)}, s32[256]{0:T(256)}, u32[]{:S(2)}) copy-start(s32[256]{0:T(256)} %param.3) | copy-start | bytes 3076
  56.9 5.2 %collective-permute-start = (bf16[512,768]{1,0:T(8,128)(2,1)S(1)}, bf16[512,768]{1,0:T(8,128)(2,1)S(1)}, u32[]{:S(2)}, u32[]{:S(2)}) collective-permute-start(bf16[512,768]{1,0:T(8,128)(2,1)S(1)} %bitcast.8), channel_id=1, source_target_pairs={{0,1},{1,0},{2,3},{3,2},{4,5},{5,4},{6,7},{7,6},{8,9},{9,8},{10,11... | collective-permute-start | bytes 2359304 | tf_op jit(solution)/shard_map/ppermute | solution.py:144

commit v5 on v4

--- a/solution.py
+++ b/solution.py
@@ -9,6 +9,7 @@
 
 CAPACITY = 8
 LANES = 128
+BLOCK = 256
 LOWEST = -1e30
 ROWS_FIRST = 47
 ANSWERS_FIRST = 34
@@ -67,8 +68,12 @@
 
 def cross_kernel(turn, own_ref, other_ref, best_ref, message_ref):
     own, other = own_ref[...], other_ref[...]
-    scores = jnp.where(present(other), scores_of(other, own), LOWEST)
-    best = jnp.maximum(best_ref[...], jnp.max(scores, axis=0, keepdims=True))
+    usable = present(other)
+    found = []
+    for start in range(0, own.shape[0], BLOCK):
+        scores = scores_of(other, own[start : start + BLOCK])
+        found.append(jnp.max(jnp.where(usable, scores, LOWEST), axis=0, keepdims=True))
+    best = jnp.maximum(best_ref[...], jnp.concatenate(found, axis=1))
     shape = message_ref.shape
     source, lane = turned(iota(shape, 0), turn, shape[0]), iota(shape, 1)
     message = jnp.zeros(shape, jnp.float32)

time: 81.5 us -> 81.5 us (level)
  no operation moved by 1% of the time
where the time goes in v5:
time: 81.5 us; the launch traced here: 81 us
  blocking collectives  72.8 us (89%)
  starting transfers between devices  3.29 us (4%)
  Pallas kernels  2.61 us (3%)
  waiting for transfers between devices  1.27 us (2%)
  local copies, waits for them, and re-layouts  0.95 us (1%)
    all_to_all x2, blocking collectives, exchange(): lax.all_to_all(blocks, 'dev', 0, 0, axis_index_groups=groups(first, chips...  72.8 us
    ppermute x1, starting transfers between devices, body(): other = lax.ppermute(own, 'dev', [(d, d ^ 1) for d in range(devices)])  3.29 us
    pallas_call x5, Pallas kernels, call(): pl.pallas_call(kernel, out_shape=outs, in_specs=[whole] * len(args), out_...  2.61 us
  transfers between devices with their start and end apart: 1, of which 1 were waited for; matrix products, arithmetic and copies ran while one was open for 0% of the time, Pallas kernels for 1%

profile of v5, /device:TPU:1, one launch (start us, length us, event | category | flops | bytes accessed | tf_op | source)
XLA Modules:
  0.0 81.0 jit_solution(15857434397080160174)
XLA Ops:
  0.0 0.0 copy-start
  0.0 0.0 copy-start.1
  0.1 0.9 %copy-done = bf16[256,768]{1,0:T(8,128)(2,1)S(1)} copy-done((bf16[256,768]{1,0:T(8,128)(2,1)S(1)}, bf16[256,768]{1,0:T(8,128)(2,1)}, u32[]{:S(2)}) %copy-start) | copy-done | bytes 393240
  1.0 0.0 copy-done.1
  1.0 0.6 shard_map.29
  1.6 55.3 %all_to_all.10 = bf16[64,8,768]{2,1,0:T(8,128)(2,1)S(1)} all-to-all(bf16[64,8,768]{2,1,0:T(8,128)(2,1)S(1)} %bitcast.11), channel_id=1, replica_groups={{94,96,98,100,102,104,106,108,110,112,114,116,118,120,122,124,126,0,2,4..., dimensions={0} | all-to-all | bytes 1572864 | tf_op jit(solution)/shard_map/all_to_all | solution.py:133
  56.9 3.3 %collective-permute-start = (bf16[512,768]{1,0:T(8,128)(2,1)S(1)}, bf16[512,768]{1,0:T(8,128)(2,1)S(1)}, u32[]{:S(2)}, u32[]{:S(2)}) collective-permute-start(bf16[512,768]{1,0:T(8,128)(2,1)S(1)} %bitcast.8), channel_id=1, source_target_pairs={{0,1},{1,0},{2,3},{3,2},{4,5},{5,4},{6,7},{7,6},{8,9},{9,8},{10,11... | collective-permute-start | bytes 2359304 | tf_op jit(solution)/shard_map/ppermute | solution.py:149
  60.2 0.6 shard_map.30.best_ref
  60.8 1.3 %collective-permute-done.other_ref = bf16[512,768]{1,0:T(8,128)(2,1)S(1)} collective-permute-done((bf16[512,768]{1,0:T(8,128)(2,1)S(1)}, bf16[512,768]{1,0:T(8,128)(2,1)S(1)}, u32[]{:S(2)}, u32[]{:S(2)}) %collective-permute-start) | collective-permute-done | bytes 786464 | tf_op jit(solution)/shard_map/ppermute | solution.py:149
  62.1 0.6 shard_map.31
  62.7 17.5 %all_to_all.11 = f32[64,1,128]{2,1,0:T(1,128)S(1)} all-to-all(f32[64,1,128]{2,1,0:T(1,128)S(1)} %bitcast.12), channel_id=1, replica_groups={{68,70,72,74,76,78,80,82,84,86,88,90,92,94,96,98,100,102,104,106,108,11..., dimensions={0} | all-to-all | bytes 65536 | tf_op jit(solution)/shard_map/all_to_all | solution.py:133
  80.2 0.8 shard_map.32
  (1 shorter events, 0.0 us)
Async XLA Ops:
  0.0 1.0 %copy-start = (bf16[256,768]{1,0:T(8,128)(2,1)S(1)}, bf16[256,768]{1,0:T(8,128)(2,1)}, u32[]{:S(2)}) copy-start(bf16[256,768]{1,0:T(8,128)(2,1)} %rows_ref.1) | copy-start | bytes 1179652
  0.0 1.0 %copy-start.1 = (s32[256]{0:T(256)S(1)}, s32[256]{0:T(256)}, u32[]{:S(2)}) copy-start(s32[256]{0:T(256)} %param.3) | copy-start | bytes 3076
  56.9 5.2 %collective-permute-start = (bf16[512,768]{1,0:T(8,128)(2,1)S(1)}, bf16[512,768]{1,0:T(8,128)(2,1)S(1)}, u32[]{:S(2)}, u32[]{:S(2)}) collective-permute-start(bf16[512,768]{1,0:T(8,128)(2,1)S(1)} %bitcast.8), channel_id=1, source_target_pairs={{0,1},{1,0},{2,3},{3,2},{4,5},{5,4},{6,7},{7,6},{8,9},{9,8},{10,11... | collective-permute-start | bytes 2359304 | tf_op jit(solution)/shard_map/ppermute | solution.py:149
